TPU v7x, 256 devices: a whole 4x4x8 slice. The times are simulated.
256 devices in a mesh: pipe: 8 (over x, core), neuron: 32 (over y, z).
Axes of the slice: x: 4, y: 4, z: 8, core: 2. Of those that a mesh axis runs over, the one named last changes fastest.
Arguments:
- inputs: bfloat16 [2, 128, 65536], P(None, None, 'neuron'), may hold values from -6 to 6
- weights: bfloat16 [8, 512, 16, 128, 128], P('pipe', 'neuron'), may hold values from -0.1875 to 0.1875
- pattern: int32 [8, 512, 16], P('pipe', 'neuron'), may hold values from 0 to 511, as said below
- bias: float32 [8, 65536], P('pipe', 'neuron'), may hold values from -1.5 to 1.5
Outputs:
- activations: bfloat16 [8, 2, 128, 65536], P('pipe', None, None, 'neuron')
Inputs may be any that keep to these rules, and one draw needn't show every extreme that they name: `pattern`: entry [l, j, k] names an input block that lies in the group of 16 blocks holding output block j (groups j // 16), or in one of the two groups beside it, counted cyclically over the 32 groups; entries of one row may repeat.
All inputs are finite; a program needn't handle non-finite values.
Results may differ from a plain program's by a relative error of at most 0.015.
Values may be sent and summed in bfloat16 or wider, within the bound.
A program may use at most 128 MiB of HBM per device.

v0:
```python
import jax
import jax.numpy as jnp
from jax import lax
from jax.sharding import PartitionSpec as P


def with_halo(cells, sides, width):
    for axis, dim in sides:
        count = lax.axis_size(axis)
        head = lax.slice_in_dim(cells, 0, width, axis=dim)
        tail = lax.slice_in_dim(cells, cells.shape[dim] - width, cells.shape[dim], axis=dim)
        cells = jnp.concatenate(
            [
                lax.ppermute(tail, axis, [(i, (i + 1) % count) for i in range(count)]),
                cells,
                lax.ppermute(head, axis, [((i + 1) % count, i) for i in range(count)]),
            ],
            axis=dim,
        )
    return cells


def passed_along(shard, axis, by):
    length = lax.axis_size(axis)
    pairs = [(i, i + by) for i in range(length) if 0 <= i + by < length]
    return lax.ppermute(shard, axis, pairs)


def per_device(inputs, weights, pattern, bias):
    blocks_here = weights.shape[1]
    width = weights.shape[3]
    columns = blocks_here * width
    group_count = lax.axis_size("neuron")
    total_blocks = blocks_here * group_count
    member = lax.axis_index("neuron")
    section = lax.axis_index("pipe")
    sections = lax.axis_size("pipe")
    local_ids = jnp.mod(pattern[0] - (member - 1) * blocks_here, total_blocks).reshape(-1)
    micro, rows = (inputs.shape[0], inputs.shape[1])
    rounds = micro // micro

    def layer_apply(extended):
        batch = extended.shape[0]
        tiles = extended.reshape(batch * rows, 3 * blocks_here, width)
        picked = jnp.take(tiles, local_ids, axis=1).reshape(batch * rows, blocks_here, -1, width)
        summed = jnp.einsum(
            "rjkc,jkcd->rjd", picked, weights[0], preferred_element_type=jnp.float32
        )
        summed = summed.reshape(batch, rows, columns) + bias[0]
        return jnp.maximum(summed, 0.0).astype(jnp.bfloat16)

    def spare_layer(extended):
        return jnp.zeros((extended.shape[0], rows, columns), jnp.bfloat16)

    def plan_slot(step):
        offset = step - section
        active = jnp.logical_and(offset >= 0, offset < rounds)
        return (active, jnp.clip(offset, 0, rounds - 1))

    def store(outputs, active, result):
        return jnp.where(active, result, outputs)

    outputs_init = jnp.zeros((micro, rows, columns), jnp.bfloat16)

    def tick(step, carry):
        received, outputs = carry
        active, slot = plan_slot(step)
        slab = jnp.where(section == 0, inputs, received)
        extended = with_halo(slab, (("neuron", 2),), columns)
        result = lax.cond(active, layer_apply, spare_layer, extended)
        outputs = store(outputs, active, result)
        received = passed_along(result, "pipe", 1)
        return (received, outputs)

    start = jnp.zeros((micro, rows, columns), jnp.bfloat16)
    final = lax.fori_loop(0, rounds + sections - 1, tick, (start, outputs_init))
    return final[1][None]


def solution(mesh):
    in_specs = (
        P(None, None, "neuron"),
        P("pipe", "neuron", None, None, None),
        P("pipe", "neuron", None),
        P("pipe", "neuron"),
    )
    out_specs = P("pipe", None, None, "neuron")
    return jax.shard_map(
        per_device, mesh=mesh, in_specs=in_specs, out_specs=out_specs, check_vma=False
    )
```

profile of v0, /device:TPU:7, one launch (start us, length us, event | category | flops | bytes accessed | tf_op | source)
XLA Modules:
  0.0 453.7 jit_solution(14239581671576209288)
XLA Ops:
  0.9 452.8 %while.17 = (s32[]{:T(128)}, bf16[2,128,2048]{2,1,0:T(8,128)(2,1)S(1)}, bf16[2,128,2048]{2,1,0:T(8,128)(2,1)}, s32[]{:T(128)}, pred[]{:T(512)}, /*index=5*/bf16[...) while((s32[]{:T(128)}, ...), condition=%wide.region_3.4_spmd.clone, body=%wide.region_0.3_spmd.clone.sunk | while | flops 2168458496 | bytes 110152024 | solution.py:76
  1.1 8.1 %collective-permute-start = (bf16[2,128,2048]{2,1,0:T(8,128)(2,1)S(1)}, bf16[2,128,2048]{2,1,0:T(8,128)(2,1)S(1)}, u32[]{:S(2)}, u32[]{:S(2)}) collective-permute-start(bf16[2,128,2048]{2,1,0:T(8,128)(2,1)S(1)} %broadcast_select_fusion.2), channel_id=1, source_target_pairs={{1,0},{2,1},{3,2},{4,3},{5,4},{6,5},{7,6},{8,7},{9,8},{10,9},{11,1... | collective-permute-start | bytes 3145736 | tf_op jit(solution)/shard_map/while/body/eval_jaxpr/ppermute | solution.py:16
  9.2 21.8 %collective-permute-done = bf16[2,128,2048]{2,1,0:T(8,128)(2,1)S(1)} collective-permute-done((bf16[2,128,2048]{2,1,0:T(8,128)(2,1)S(1)}, bf16[2,128,2048]{2,1,0:T(8,128)(2,1)S(1)}, u32[]{:S(2)}, u32[]{:S(2)}) %collective-permute-start) | collective-permute-done | bytes 1048608 | tf_op jit(solution)/shard_map/while/body/eval_jaxpr/ppermute | solution.py:16
  31.0 5.2 %collective-permute-done.1 = bf16[2,128,2048]{2,1,0:T(8,128)(2,1)S(1)} collective-permute-done((bf16[2,128,2048]{2,1,0:T(8,128)(2,1)S(1)}, bf16[2,128,2048]{2,1,0:T(8,128)(2,1)S(1)}, u32[]{:S(2)}, u32[]{:S(2)}) %collective-permute-start.1) | collective-permute-done | bytes 1048608 | tf_op jit(solution)/shard_map/while/body/eval_jaxpr/ppermute | solution.py:14
  36.7 1.3 collective-permute-start.2
  39.1 3.5 collective-permute-done.2
  42.8 1.5 collective-permute-start.1
  44.2 12.2 %collective-permute-done = bf16[2,128,2048]{2,1,0:T(8,128)(2,1)S(1)} collective-permute-done((bf16[2,128,2048]{2,1,0:T(8,128)(2,1)S(1)}, bf16[2,128,2048]{2,1,0:T(8,128)(2,1)S(1)}, u32[]{:S(2)}, u32[]{:S(2)}) %collective-permute-start) | collective-permute-done | bytes 1048608 | tf_op jit(solution)/shard_map/while/body/eval_jaxpr/ppermute | solution.py:16
  56.4 3.4 collective-permute-done.1
  60.3 1.3 collective-permute-start.2
  61.6 2.3 select_select_fusion.2
  63.9 13.8 %collective-permute-done.2 = bf16[2,128,2048]{2,1,0:T(8,128)(2,1)S(1)} collective-permute-done((bf16[2,128,2048]{2,1,0:T(8,128)(2,1)S(1)}, bf16[2,128,2048]{2,1,0:T(8,128)(2,1)S(1)}, u32[]{:S(2)}, u32[]{:S(2)}) %collective-permute-start.2) | collective-permute-done | bytes 1048608 | tf_op jit(solution)/shard_map/while/body/eval_jaxpr/ppermute | solution.py:26
  78.0 1.5 collective-permute-start.1
  79.4 12.5 %collective-permute-done = bf16[2,128,2048]{2,1,0:T(8,128)(2,1)S(1)} collective-permute-done((bf16[2,128,2048]{2,1,0:T(8,128)(2,1)S(1)}, bf16[2,128,2048]{2,1,0:T(8,128)(2,1)S(1)}, u32[]{:S(2)}, u32[]{:S(2)}) %collective-permute-start) | collective-permute-done | bytes 1048608 | tf_op jit(solution)/shard_map/while/body/eval_jaxpr/ppermute | solution.py:16
  91.9 3.1 collective-permute-done.1
  95.4 1.3 collective-permute-start.2
  96.8 2.3 select_select_fusion.2
  99.1 19.3 %collective-permute-done.2 = bf16[2,128,2048]{2,1,0:T(8,128)(2,1)S(1)} collective-permute-done((bf16[2,128,2048]{2,1,0:T(8,128)(2,1)S(1)}, bf16[2,128,2048]{2,1,0:T(8,128)(2,1)S(1)}, u32[]{:S(2)}, u32[]{:S(2)}) %collective-permute-start.2) | collective-permute-done | bytes 1048608 | tf_op jit(solution)/shard_map/while/body/eval_jaxpr/ppermute | solution.py:26
  118.5 1.5 collective-permute-start.1
  120.0 12.2 %collective-permute-done = bf16[2,128,2048]{2,1,0:T(8,128)(2,1)S(1)} collective-permute-done((bf16[2,128,2048]{2,1,0:T(8,128)(2,1)S(1)}, bf16[2,128,2048]{2,1,0:T(8,128)(2,1)S(1)}, u32[]{:S(2)}, u32[]{:S(2)}) %collective-permute-start) | collective-permute-done | bytes 1048608 | tf_op jit(solution)/shard_map/while/body/eval_jaxpr/ppermute | solution.py:16
  132.2 3.4 collective-permute-done.1
  137.4 2.3 select_select_fusion.2
  139.7 15.9 %collective-permute-done.2 = bf16[2,128,2048]{2,1,0:T(8,128)(2,1)S(1)} collective-permute-done((bf16[2,128,2048]{2,1,0:T(8,128)(2,1)S(1)}, bf16[2,128,2048]{2,1,0:T(8,128)(2,1)S(1)}, u32[]{:S(2)}, u32[]{:S(2)}) %collective-permute-start.2) | collective-permute-done | bytes 1048608 | tf_op jit(solution)/shard_map/while/body/eval_jaxpr/ppermute | solution.py:26
  155.8 1.5 collective-permute-start.1
  157.2 12.2 %collective-permute-done = bf16[2,128,2048]{2,1,0:T(8,128)(2,1)S(1)} collective-permute-done((bf16[2,128,2048]{2,1,0:T(8,128)(2,1)S(1)}, bf16[2,128,2048]{2,1,0:T(8,128)(2,1)S(1)}, u32[]{:S(2)}, u32[]{:S(2)}) %collective-permute-start) | collective-permute-done | bytes 1048608 | tf_op jit(solution)/shard_map/while/body/eval_jaxpr/ppermute | solution.py:16
  169.4 3.4 collective-permute-done.1
  174.6 2.3 select_select_fusion.2
  176.9 13.6 %collective-permute-done.2 = bf16[2,128,2048]{2,1,0:T(8,128)(2,1)S(1)} collective-permute-done((bf16[2,128,2048]{2,1,0:T(8,128)(2,1)S(1)}, bf16[2,128,2048]{2,1,0:T(8,128)(2,1)S(1)}, u32[]{:S(2)}, u32[]{:S(2)}) %collective-permute-start.2) | collective-permute-done | bytes 1048608 | tf_op jit(solution)/shard_map/while/body/eval_jaxpr/ppermute | solution.py:26
  190.7 1.5 collective-permute-start.1
  192.2 12.2 %collective-permute-done = bf16[2,128,2048]{2,1,0:T(8,128)(2,1)S(1)} collective-permute-done((bf16[2,128,2048]{2,1,0:T(8,128)(2,1)S(1)}, bf16[2,128,2048]{2,1,0:T(8,128)(2,1)S(1)}, u32[]{:S(2)}, u32[]{:S(2)}) %collective-permute-start) | collective-permute-done | bytes 1048608 | tf_op jit(solution)/shard_map/while/body/eval_jaxpr/ppermute | solution.py:16
  204.4 3.4 collective-permute-done.1
  209.5 2.3 select_select_fusion.2
  211.8 13.6 %collective-permute-done.2 = bf16[2,128,2048]{2,1,0:T(8,128)(2,1)S(1)} collective-permute-done((bf16[2,128,2048]{2,1,0:T(8,128)(2,1)S(1)}, bf16[2,128,2048]{2,1,0:T(8,128)(2,1)S(1)}, u32[]{:S(2)}, u32[]{:S(2)}) %collective-permute-start.2) | collective-permute-done | bytes 1048608 | tf_op jit(solution)/shard_map/while/body/eval_jaxpr/ppermute | solution.py:26
  225.7 1.5 collective-permute-start.1
  227.2 12.2 %collective-permute-done = bf16[2,128,2048]{2,1,0:T(8,128)(2,1)S(1)} collective-permute-done((bf16[2,128,2048]{2,1,0:T(8,128)(2,1)S(1)}, bf16[2,128,2048]{2,1,0:T(8,128)(2,1)S(1)}, u32[]{:S(2)}, u32[]{:S(2)}) %collective-permute-start) | collective-permute-done | bytes 1048608 | tf_op jit(solution)/shard_map/while/body/eval_jaxpr/ppermute | solution.py:16
  239.3 3.4 collective-permute-done.1
  243.2 1.3 collective-permute-start.2
  244.5 2.3 select_select_fusion.2
  246.8 158.1 %collective-permute-done.2 = bf16[2,128,2048]{2,1,0:T(8,128)(2,1)S(1)} collective-permute-done((bf16[2,128,2048]{2,1,0:T(8,128)(2,1)S(1)}, bf16[2,128,2048]{2,1,0:T(8,128)(2,1)S(1)}, u32[]{:S(2)}, u32[]{:S(2)}) %collective-permute-start.2) | collective-permute-done | bytes 1048608 | tf_op jit(solution)/shard_map/while/body/eval_jaxpr/ppermute | solution.py:26
  405.1 1.5 collective-permute-start.1
  406.6 12.2 %collective-permute-done = bf16[2,128,2048]{2,1,0:T(8,128)(2,1)S(1)} collective-permute-done((bf16[2,128,2048]{2,1,0:T(8,128)(2,1)S(1)}, bf16[2,128,2048]{2,1,0:T(8,128)(2,1)S(1)}, u32[]{:S(2)}, u32[]{:S(2)}) %collective-permute-start) | collective-permute-done | bytes 1048608 | tf_op jit(solution)/shard_map/while/body/eval_jaxpr/ppermute | solution.py:16
  418.8 3.4 collective-permute-done.1
  422.5 26.6 %conditional.3 = (bf16[2,128,2048]{2,1,0:T(8,128)(2,1)S(1)}) conditional(s32[]{:T(128)} %convert_element_type.14, () %tuple.46, (s32[256]{0:T(256)S(1)}, bf16[2,128,6144]{2,1,0:T(8,128)(2,1)S(1)}, bf16[1,16,16,128,128]{4,3,2,1,0:T(8,128)(2,1)}, f32[1,2048]{1,0:T(1,128)S(1)}) %tuple.53), branch_computations={%region_1.1_spmd, %region_2.2_spmd} | conditional | flops 2157448448 | bytes 84953096 | solution.py:70
  424.1 9.7 %gather_fusion = bf16[256,256,128]{2,1,0:T(8,128)(2,1)} fusion(bf16[256,48,128]{2,0,1:T(8,128)(2,1)S(1)} %copy.7, s32[1024]{0:T(1024)S(1)} %pad_clamp_fusion), kind=kCustom, calls=%fused_computation | custom fusion | bytes 33555456 | tf_op jit(solution)/shard_map/while/body/eval_jaxpr/cond/branch_1_fun/jit(_take)/gather | solution.py:45
  433.9 10.6 %fusion.5 = f32[256,16,128]{2,0,1:T(8,128)S(1)} fusion(bf16[1,16,16,128,128]{4,3,2,1,0:T(8,128)(2,1)} %get-tuple-element.188, bf16[256,16,16,128]{3,0,2,1:T(8,128)(2,1)} %bitcast.18, pred[16,16]{1,0:T(8,128)(4,1)S(1)} %broadcast_in_dim.12), kind=kOutput, calls=%fused_computation.7 | convolution fusion | flops 2155872256 | bytes 27263232 | tf_op jit(solution)/shard_map/while/body/eval_jaxpr/cond/branch_1_fun/rjkc,jkcd->rjd/dot_general | solution.py:46
  445.8 1.5 reshape.19
  447.3 1.8 maximum_convert_fusion
  450.5 2.3 select_select_fusion.2
  (72 shorter events, 16.5 us)
Async XLA Ops:
  0.9 35.6 %copy-start = (f32[1,2048]{1,0:T(1,128)S(1)}, f32[1,2048]{1,0:T(1,128)}, u32[]{:S(2)}) copy-start(f32[1,2048]{1,0:T(1,128)} %get-tuple-element.335) | copy-start | bytes 24580 | tf_op jit(solution)/shard_map/while
  1.1 29.9 %collective-permute-start = (bf16[2,128,2048]{2,1,0:T(8,128)(2,1)S(1)}, bf16[2,128,2048]{2,1,0:T(8,128)(2,1)S(1)}, u32[]{:S(2)}, u32[]{:S(2)}) collective-permute-start(bf16[2,128,2048]{2,1,0:T(8,128)(2,1)S(1)} %broadcast_select_fusion.2), channel_id=1, source_target_pairs={{1,0},{2,1},{3,2},{4,3},{5,4},{6,5},{7,6},{8,7},{9,8},{10,9},{11,1... | collective-permute-start | bytes 3145736 | tf_op jit(solution)/shard_map/while/body/eval_jaxpr/ppermute | solution.py:16
  9.2 27.0 %collective-permute-start.1 = (bf16[2,128,2048]{2,1,0:T(8,128)(2,1)S(1)}, bf16[2,128,2048]{2,1,0:T(8,128)(2,1)S(1)}, u32[]{:S(2)}, u32[]{:S(2)}) collective-permute-start(bf16[2,128,2048]{2,1,0:T(8,128)(2,1)S(1)} %broadcast_select_fusion.2), channel_id=1, source_target_pairs={{0,1},{1,2},{2,3},{3,4},{4,5},{5,6},{6,7},{7,8},{8,9},{9,10},{10,1... | collective-permute-start | bytes 3145736 | tf_op jit(solution)/shard_map/while/body/eval_jaxpr/ppermute | solution.py:14
  36.7 5.9 %collective-permute-start.2 = (bf16[2,128,2048]{2,1,0:T(8,128)(2,1)S(1)}, bf16[2,128,2048]{2,1,0:T(8,128)(2,1)S(1)}, u32[]{:S(2)}, u32[]{:S(2)}) collective-permute-start(bf16[2,128,2048]{2,1,0:T(8,128)(2,1)S(1)} %get-tuple-element.338), channel_id=1, source_target_pairs={{0,32},{32,64},{64,96},{96,128},{128,160},{160,192},{192,224},{1,3... | collective-permute-start | bytes 3145736 | tf_op jit(solution)/shard_map/while/body/eval_jaxpr/ppermute | solution.py:26
  42.6 17.6 %copy-start = (f32[1,2048]{1,0:T(1,128)S(1)}, f32[1,2048]{1,0:T(1,128)}, u32[]{:S(2)}) copy-start(f32[1,2048]{1,0:T(1,128)} %get-tuple-element.335) | copy-start | bytes 24580 | tf_op jit(solution)/shard_map/while
  42.7 13.7 %collective-permute-start = (bf16[2,128,2048]{2,1,0:T(8,128)(2,1)S(1)}, bf16[2,128,2048]{2,1,0:T(8,128)(2,1)S(1)}, u32[]{:S(2)}, u32[]{:S(2)}) collective-permute-start(bf16[2,128,2048]{2,1,0:T(8,128)(2,1)S(1)} %broadcast_select_fusion.2), channel_id=1, source_target_pairs={{1,0},{2,1},{3,2},{4,3},{5,4},{6,5},{7,6},{8,7},{9,8},{10,9},{11,1... | collective-permute-start | bytes 3145736 | tf_op jit(solution)/shard_map/while/body/eval_jaxpr/ppermute | solution.py:16
  42.8 17.0 %collective-permute-start.1 = (bf16[2,128,2048]{2,1,0:T(8,128)(2,1)S(1)}, bf16[2,128,2048]{2,1,0:T(8,128)(2,1)S(1)}, u32[]{:S(2)}, u32[]{:S(2)}) collective-permute-start(bf16[2,128,2048]{2,1,0:T(8,128)(2,1)S(1)} %broadcast_select_fusion.2), channel_id=1, source_target_pairs={{0,1},{1,2},{2,3},{3,4},{4,5},{5,6},{6,7},{7,8},{8,9},{9,10},{10,1... | collective-permute-start | bytes 3145736 | tf_op jit(solution)/shard_map/while/body/eval_jaxpr/ppermute | solution.py:14
  60.3 17.5 %collective-permute-start.2 = (bf16[2,128,2048]{2,1,0:T(8,128)(2,1)S(1)}, bf16[2,128,2048]{2,1,0:T(8,128)(2,1)S(1)}, u32[]{:S(2)}, u32[]{:S(2)}) collective-permute-start(bf16[2,128,2048]{2,1,0:T(8,128)(2,1)S(1)} %get-tuple-element.338), channel_id=1, source_target_pairs={{0,32},{32,64},{64,96},{96,128},{128,160},{160,192},{192,224},{1,3... | collective-permute-start | bytes 3145736 | tf_op jit(solution)/shard_map/while/body/eval_jaxpr/ppermute | solution.py:26
  77.7 17.6 %copy-start = (f32[1,2048]{1,0:T(1,128)S(1)}, f32[1,2048]{1,0:T(1,128)}, u32[]{:S(2)}) copy-start(f32[1,2048]{1,0:T(1,128)} %get-tuple-element.335) | copy-start | bytes 24580 | tf_op jit(solution)/shard_map/while
  77.9 14.0 %collective-permute-start = (bf16[2,128,2048]{2,1,0:T(8,128)(2,1)S(1)}, bf16[2,128,2048]{2,1,0:T(8,128)(2,1)S(1)}, u32[]{:S(2)}, u32[]{:S(2)}) collective-permute-start(bf16[2,128,2048]{2,1,0:T(8,128)(2,1)S(1)} %broadcast_select_fusion.2), channel_id=1, source_target_pairs={{1,0},{2,1},{3,2},{4,3},{5,4},{6,5},{7,6},{8,7},{9,8},{10,9},{11,1... | collective-permute-start | bytes 3145736 | tf_op jit(solution)/shard_map/while/body/eval_jaxpr/ppermute | solution.py:16
  78.0 17.0 %collective-permute-start.1 = (bf16[2,128,2048]{2,1,0:T(8,128)(2,1)S(1)}, bf16[2,128,2048]{2,1,0:T(8,128)(2,1)S(1)}, u32[]{:S(2)}, u32[]{:S(2)}) collective-permute-start(bf16[2,128,2048]{2,1,0:T(8,128)(2,1)S(1)} %broadcast_select_fusion.2), channel_id=1, source_target_pairs={{0,1},{1,2},{2,3},{3,4},{4,5},{5,6},{6,7},{7,8},{8,9},{9,10},{10,1... | collective-permute-start | bytes 3145736 | tf_op jit(solution)/shard_map/while/body/eval_jaxpr/ppermute | solution.py:14
  95.4 22.9 %collective-permute-start.2 = (bf16[2,128,2048]{2,1,0:T(8,128)(2,1)S(1)}, bf16[2,128,2048]{2,1,0:T(8,128)(2,1)S(1)}, u32[]{:S(2)}, u32[]{:S(2)}) collective-permute-start(bf16[2,128,2048]{2,1,0:T(8,128)(2,1)S(1)} %get-tuple-element.338), channel_id=1, source_target_pairs={{0,32},{32,64},{64,96},{96,128},{128,160},{160,192},{192,224},{1,3... | collective-permute-start | bytes 3145736 | tf_op jit(solution)/shard_map/while/body/eval_jaxpr/ppermute | solution.py:26
  118.3 17.6 %copy-start = (f32[1,2048]{1,0:T(1,128)S(1)}, f32[1,2048]{1,0:T(1,128)}, u32[]{:S(2)}) copy-start(f32[1,2048]{1,0:T(1,128)} %get-tuple-element.335) | copy-start | bytes 24580 | tf_op jit(solution)/shard_map/while
  118.5 13.7 %collective-permute-start = (bf16[2,128,2048]{2,1,0:T(8,128)(2,1)S(1)}, bf16[2,128,2048]{2,1,0:T(8,128)(2,1)S(1)}, u32[]{:S(2)}, u32[]{:S(2)}) collective-permute-start(bf16[2,128,2048]{2,1,0:T(8,128)(2,1)S(1)} %broadcast_select_fusion.2), channel_id=1, source_target_pairs={{1,0},{2,1},{3,2},{4,3},{5,4},{6,5},{7,6},{8,7},{9,8},{10,9},{11,1... | collective-permute-start | bytes 3145736 | tf_op jit(solution)/shard_map/while/body/eval_jaxpr/ppermute | solution.py:16
  118.5 17.0 %collective-permute-start.1 = (bf16[2,128,2048]{2,1,0:T(8,128)(2,1)S(1)}, bf16[2,128,2048]{2,1,0:T(8,128)(2,1)S(1)}, u32[]{:S(2)}, u32[]{:S(2)}) collective-permute-start(bf16[2,128,2048]{2,1,0:T(8,128)(2,1)S(1)} %broadcast_select_fusion.2), channel_id=1, source_target_pairs={{0,1},{1,2},{2,3},{3,4},{4,5},{5,6},{6,7},{7,8},{8,9},{9,10},{10,1... | collective-permute-start | bytes 3145736 | tf_op jit(solution)/shard_map/while/body/eval_jaxpr/ppermute | solution.py:14
  136.0 19.5 %collective-permute-start.2 = (bf16[2,128,2048]{2,1,0:T(8,128)(2,1)S(1)}, bf16[2,128,2048]{2,1,0:T(8,128)(2,1)S(1)}, u32[]{:S(2)}, u32[]{:S(2)}) collective-permute-start(bf16[2,128,2048]{2,1,0:T(8,128)(2,1)S(1)} %get-tuple-element.338), channel_id=1, source_target_pairs={{0,32},{32,64},{64,96},{96,128},{128,160},{160,192},{192,224},{1,3... | collective-permute-start | bytes 3145736 | tf_op jit(solution)/shard_map/while/body/eval_jaxpr/ppermute | solution.py:26
  155.5 17.6 %copy-start = (f32[1,2048]{1,0:T(1,128)S(1)}, f32[1,2048]{1,0:T(1,128)}, u32[]{:S(2)}) copy-start(f32[1,2048]{1,0:T(1,128)} %get-tuple-element.335) | copy-start | bytes 24580 | tf_op jit(solution)/shard_map/while
  155.7 13.7 %collective-permute-start = (bf16[2,128,2048]{2,1,0:T(8,128)(2,1)S(1)}, bf16[2,128,2048]{2,1,0:T(8,128)(2,1)S(1)}, u32[]{:S(2)}, u32[]{:S(2)}) collective-permute-start(bf16[2,128,2048]{2,1,0:T(8,128)(2,1)S(1)} %broadcast_select_fusion.2), channel_id=1, source_target_pairs={{1,0},{2,1},{3,2},{4,3},{5,4},{6,5},{7,6},{8,7},{9,8},{10,9},{11,1... | collective-permute-start | bytes 3145736 | tf_op jit(solution)/shard_map/while/body/eval_jaxpr/ppermute | solution.py:16
  155.8 17.0 %collective-permute-start.1 = (bf16[2,128,2048]{2,1,0:T(8,128)(2,1)S(1)}, bf16[2,128,2048]{2,1,0:T(8,128)(2,1)S(1)}, u32[]{:S(2)}, u32[]{:S(2)}) collective-permute-start(bf16[2,128,2048]{2,1,0:T(8,128)(2,1)S(1)} %broadcast_select_fusion.2), channel_id=1, source_target_pairs={{0,1},{1,2},{2,3},{3,4},{4,5},{5,6},{6,7},{7,8},{8,9},{9,10},{10,1... | collective-permute-start | bytes 3145736 | tf_op jit(solution)/shard_map/while/body/eval_jaxpr/ppermute | solution.py:14
  173.2 17.3 %collective-permute-start.2 = (bf16[2,128,2048]{2,1,0:T(8,128)(2,1)S(1)}, bf16[2,128,2048]{2,1,0:T(8,128)(2,1)S(1)}, u32[]{:S(2)}, u32[]{:S(2)}) collective-permute-start(bf16[2,128,2048]{2,1,0:T(8,128)(2,1)S(1)} %get-tuple-element.338), channel_id=1, source_target_pairs={{0,32},{32,64},{64,96},{96,128},{128,160},{160,192},{192,224},{1,3... | collective-permute-start | bytes 3145736 | tf_op jit(solution)/shard_map/while/body/eval_jaxpr/ppermute | solution.py:26
  190.5 17.6 %copy-start = (f32[1,2048]{1,0:T(1,128)S(1)}, f32[1,2048]{1,0:T(1,128)}, u32[]{:S(2)}) copy-start(f32[1,2048]{1,0:T(1,128)} %get-tuple-element.335) | copy-start | bytes 24580 | tf_op jit(solution)/shard_map/while
  190.6 13.7 %collective-permute-start = (bf16[2,128,2048]{2,1,0:T(8,128)(2,1)S(1)}, bf16[2,128,2048]{2,1,0:T(8,128)(2,1)S(1)}, u32[]{:S(2)}, u32[]{:S(2)}) collective-permute-start(bf16[2,128,2048]{2,1,0:T(8,128)(2,1)S(1)} %broadcast_select_fusion.2), channel_id=1, source_target_pairs={{1,0},{2,1},{3,2},{4,3},{5,4},{6,5},{7,6},{8,7},{9,8},{10,9},{11,1... | collective-permute-start | bytes 3145736 | tf_op jit(solution)/shard_map/while/body/eval_jaxpr/ppermute | solution.py:16
  190.7 17.0 %collective-permute-start.1 = (bf16[2,128,2048]{2,1,0:T(8,128)(2,1)S(1)}, bf16[2,128,2048]{2,1,0:T(8,128)(2,1)S(1)}, u32[]{:S(2)}, u32[]{:S(2)}) collective-permute-start(bf16[2,128,2048]{2,1,0:T(8,128)(2,1)S(1)} %broadcast_select_fusion.2), channel_id=1, source_target_pairs={{0,1},{1,2},{2,3},{3,4},{4,5},{5,6},{6,7},{7,8},{8,9},{9,10},{10,1... | collective-permute-start | bytes 3145736 | tf_op jit(solution)/shard_map/while/body/eval_jaxpr/ppermute | solution.py:14
  208.2 17.3 %collective-permute-start.2 = (bf16[2,128,2048]{2,1,0:T(8,128)(2,1)S(1)}, bf16[2,128,2048]{2,1,0:T(8,128)(2,1)S(1)}, u32[]{:S(2)}, u32[]{:S(2)}) collective-permute-start(bf16[2,128,2048]{2,1,0:T(8,128)(2,1)S(1)} %get-tuple-element.338), channel_id=1, source_target_pairs={{0,32},{32,64},{64,96},{96,128},{128,160},{160,192},{192,224},{1,3... | collective-permute-start | bytes 3145736 | tf_op jit(solution)/shard_map/while/body/eval_jaxpr/ppermute | solution.py:26
  225.5 17.6 %copy-start = (f32[1,2048]{1,0:T(1,128)S(1)}, f32[1,2048]{1,0:T(1,128)}, u32[]{:S(2)}) copy-start(f32[1,2048]{1,0:T(1,128)} %get-tuple-element.335) | copy-start | bytes 24580 | tf_op jit(solution)/shard_map/while
  225.6 13.7 %collective-permute-start = (bf16[2,128,2048]{2,1,0:T(8,128)(2,1)S(1)}, bf16[2,128,2048]{2,1,0:T(8,128)(2,1)S(1)}, u32[]{:S(2)}, u32[]{:S(2)}) collective-permute-start(bf16[2,128,2048]{2,1,0:T(8,128)(2,1)S(1)} %broadcast_select_fusion.2), channel_id=1, source_target_pairs={{1,0},{2,1},{3,2},{4,3},{5,4},{6,5},{7,6},{8,7},{9,8},{10,9},{11,1... | collective-permute-start | bytes 3145736 | tf_op jit(solution)/shard_map/while/body/eval_jaxpr/ppermute | solution.py:16
  225.7 17.0 %collective-permute-start.1 = (bf16[2,128,2048]{2,1,0:T(8,128)(2,1)S(1)}, bf16[2,128,2048]{2,1,0:T(8,128)(2,1)S(1)}, u32[]{:S(2)}, u32[]{:S(2)}) collective-permute-start(bf16[2,128,2048]{2,1,0:T(8,128)(2,1)S(1)} %broadcast_select_fusion.2), channel_id=1, source_target_pairs={{0,1},{1,2},{2,3},{3,4},{4,5},{5,6},{6,7},{7,8},{8,9},{9,10},{10,1... | collective-permute-start | bytes 3145736 | tf_op jit(solution)/shard_map/while/body/eval_jaxpr/ppermute | solution.py:14
  243.2 161.7 %collective-permute-start.2 = (bf16[2,128,2048]{2,1,0:T(8,128)(2,1)S(1)}, bf16[2,128,2048]{2,1,0:T(8,128)(2,1)S(1)}, u32[]{:S(2)}, u32[]{:S(2)}) collective-permute-start(bf16[2,128,2048]{2,1,0:T(8,128)(2,1)S(1)} %get-tuple-element.338), channel_id=1, source_target_pairs={{0,32},{32,64},{64,96},{96,128},{128,160},{160,192},{192,224},{1,3... | collective-permute-start | bytes 3145736 | tf_op jit(solution)/shard_map/while/body/eval_jaxpr/ppermute | solution.py:26
  404.9 17.6 %copy-start = (f32[1,2048]{1,0:T(1,128)S(1)}, f32[1,2048]{1,0:T(1,128)}, u32[]{:S(2)}) copy-start(f32[1,2048]{1,0:T(1,128)} %get-tuple-element.335) | copy-start | bytes 24580 | tf_op jit(solution)/shard_map/while
  405.0 13.7 %collective-permute-start = (bf16[2,128,2048]{2,1,0:T(8,128)(2,1)S(1)}, bf16[2,128,2048]{2,1,0:T(8,128)(2,1)S(1)}, u32[]{:S(2)}, u32[]{:S(2)}) collective-permute-start(bf16[2,128,2048]{2,1,0:T(8,128)(2,1)S(1)} %broadcast_select_fusion.2), channel_id=1, source_target_pairs={{1,0},{2,1},{3,2},{4,3},{5,4},{6,5},{7,6},{8,7},{9,8},{10,9},{11,1... | collective-permute-start | bytes 3145736 | tf_op jit(solution)/shard_map/while/body/eval_jaxpr/ppermute | solution.py:16
  405.1 17.0 %collective-permute-start.1 = (bf16[2,128,2048]{2,1,0:T(8,128)(2,1)S(1)}, bf16[2,128,2048]{2,1,0:T(8,128)(2,1)S(1)}, u32[]{:S(2)}, u32[]{:S(2)}) collective-permute-start(bf16[2,128,2048]{2,1,0:T(8,128)(2,1)S(1)} %broadcast_select_fusion.2), channel_id=1, source_target_pairs={{0,1},{1,2},{2,3},{3,4},{4,5},{5,6},{6,7},{7,8},{8,9},{9,10},{10,1... | collective-permute-start | bytes 3145736 | tf_op jit(solution)/shard_map/while/body/eval_jaxpr/ppermute | solution.py:14
  449.1 4.6 %collective-permute-start.2 = (bf16[2,128,2048]{2,1,0:T(8,128)(2,1)S(1)}, bf16[2,128,2048]{2,1,0:T(8,128)(2,1)S(1)}, u32[]{:S(2)}, u32[]{:S(2)}) collective-permute-start(bf16[2,128,2048]{2,1,0:T(8,128)(2,1)S(1)} %get-tuple-element.338), channel_id=1, source_target_pairs={{0,32},{32,64},{64,96},{96,128},{128,160},{160,192},{192,224},{1,3... | collective-permute-start | bytes 3145736 | tf_op jit(solution)/shard_map/while/body/eval_jaxpr/ppermute | solution.py:26
where the time goes:
time: 454 us
  waiting for transfers between devices  375 us (83%)
  starting transfers between devices  29.2 us (6%)
  other arithmetic  23.1 us (5%)
  local copies, waits for them, and re-layouts  15.1 us (3%)
  matrix products  10.6 us (2%)
    ppermute x8, waiting for transfers between devices, passed_along(): return lax.ppermute(shard, axis, pairs)  239 us
    ppermute x8, waiting for transfers between devices, with_halo(): lax.ppermute(head, axis, [((i + 1) % count, i) for i in range(count)])  107 us
    ppermute x8, waiting for transfers between devices, with_halo(): lax.ppermute(tail, axis, [(i, (i + 1) % count) for i in range(count)])  28.8 us
    select_n x8, other arithmetic, store(): return jnp.where(active, result, outputs)  17.3 us
    dot_general x1, matrix products, layer_apply(): jnp.einsum('rjkc,jkcd->rjd', picked, weights[0], preferred_element_type=j...  10.6 us
    ppermute x8, starting transfers between devices, passed_along(): return lax.ppermute(shard, axis, pairs)  10.3 us
    ppermute x8, starting transfers between devices, with_halo(): lax.ppermute(tail, axis, [(i, (i + 1) % count) for i in range(count)])  10.2 us
    gather x1, local copies, waits for them, and re-layouts, layer_apply(): jnp.take(tiles, local_ids, axis=1)  9.73 us
  transfers between devices with their start and end apart: 24, of which 24 were waited for; matrix products, arithmetic and copies ran while one was open for 4% of the time, Pallas kernels for 0%

commit v1 on v0

v1 whole, which is shorter than its diff:
```python
import functools

import jax
import jax.numpy as jnp
from jax import lax
from jax.experimental import pallas as pl
from jax.experimental.pallas import tpu as pltpu
from jax.sharding import PartitionSpec as P

MESH = pl.DeviceIdType.MESH
CHUNK = 16
PIECES = 1
DIRECT_HEAD = 0
DIRECT_TAIL = 0
DIRECT_EDGE = 0
FIRST_AHEAD = 6
EVEN_AHEAD = 3
PASS_AT = 0


def kernel(
    sections, groups, chunks, rows, blocks, entries, width, pieces,
    pattern_ref, bias_ref, x_ref, w_ref, out_ref,
    ids, landing, work, held, result,
    w_sem, in_sem, own_sem, side_sem, pass_sem, send_sem, out_sem,
):
    section = lax.axis_index("pipe")
    group = lax.axis_index("neuron")
    right = lax.rem(group + 1, groups)
    left = lax.rem(group + groups - 1, groups)
    even = lax.rem(section, 2) == 0
    first = section == 0
    later_even = jnp.logical_and(even, section > 0)
    odd = jnp.logical_not(even)
    odd_sends = jnp.logical_and(odd, section < sections - 1)
    per_piece = blocks // pieces
    span = per_piece * width

    def signal(barrier, to_section, to_group):
        pl.semaphore_signal(
            barrier, inc=1, device_id={"pipe": to_section, "neuron": to_group}, device_id_type=MESH
        )

    def weight_copy(j):
        return pltpu.make_async_copy(w_ref.at[j], held.at[j], w_sem.at[j])

    for j in range(blocks):
        weight_copy(j).start()

    beside = (group, left, right)
    any_direct = DIRECT_HEAD + DIRECT_TAIL + DIRECT_EDGE > 0

    barrier = pltpu.get_barrier_semaphore()

    @pl.when(even)
    def _():
        signal(barrier, section, left)
        signal(barrier, section, right)
        for to in beside:
            signal(barrier, section + 1, to)

    @pl.when(later_even)
    def _():
        for to in beside if any_direct else (group,):
            signal(barrier, section - 1, to)

    @pl.when(odd)
    def _():
        for to in beside:
            signal(barrier, section - 1, to)

    @pl.when(odd_sends)
    def _():
        for to in beside if any_direct else (group,):
            signal(barrier, section + 1, to)

    base = (group - 1) * blocks
    total = groups * blocks

    @pl.loop(0, blocks)
    def _(j):
        for k in range(entries):
            near = lax.rem(pattern_ref[j, k] - base + total, total)
            ids[j, k] = jnp.minimum(near, 3 * blocks - 1)

    @pl.when(first)
    def _():
        pl.semaphore_wait(barrier, 5)

    @pl.when(later_even)
    def _():
        pl.semaphore_wait(barrier, 8 if any_direct else 6)

    @pl.when(odd_sends)
    def _():
        pl.semaphore_wait(barrier, 6 if any_direct else 4)

    @pl.when(jnp.logical_and(odd, section == sections - 1))
    def _():
        pl.semaphore_wait(barrier, 3)

    def row_range(c):
        return pl.ds(pl.multiple_of(c * rows, rows), rows)

    def cols(p):
        return pl.ds(p * span, span)

    def load_copy(c):
        return pltpu.make_async_copy(x_ref.at[row_range(c)], landing.at[c, 1], in_sem.at[c])

    def remote(src, dst, send, recv, to_section, to_group):
        return pltpu.make_async_remote_copy(
            src_ref=src, dst_ref=dst, send_sem=send, recv_sem=recv,
            device_id={"pipe": to_section, "neuron": to_group}, device_id_type=MESH,
        )

    def pass_copy(c, p, side):
        return remote(
            landing.at[c, 1, :, cols(p)], landing.at[c, 2 * side, :, cols(p)],
            pass_sem.at[c, p, side], side_sem.at[c, p, side], section, (right, left)[side],
        )

    def down_copy(c, p):
        return remote(
            result.at[c, :, cols(p)], landing.at[c, 1, :, cols(p)],
            send_sem.at[c, p, 2], own_sem.at[c, p], section + 1, group,
        )

    def down_side_copy(c, p, side):
        return remote(
            result.at[c, :, cols(p)], landing.at[c, 2 * side, :, cols(p)],
            send_sem.at[c, p, side], side_sem.at[c, p, side], section + 1, (right, left)[side],
        )

    def out_copy(c):
        return pltpu.make_async_copy(result.at[c], out_ref.at[row_range(c)], out_sem.at[c])

    def goes_direct(c, side):
        yes = jnp.logical_or(c < DIRECT_HEAD, c >= chunks - DIRECT_TAIL)
        if DIRECT_EDGE:
            border = (group, left)[side]
            yes = jnp.logical_or(yes, lax.rem(border, DIRECT_EDGE) == DIRECT_EDGE - 1)
        return yes

    def passes(c, side):
        return jnp.logical_not(goes_direct(c, side))

    def sends_side(c, side):
        return jnp.logical_or(even, jnp.logical_and(odd_sends, goes_direct(c, side)))

    def pass_first(c):
        load_copy(c).wait()
        for p in range(pieces):
            for side in range(2):
                pass_copy(c, p, side).start()

    def pass_even(c):
        @pl.when(jnp.logical_and(c >= DIRECT_HEAD, c < chunks - DIRECT_TAIL))
        def _():
            for p in range(pieces):
                down_copy(c, p).wait_recv()
                for side in range(2):
                    @pl.when(passes(c, side))
                    def _():
                        pass_copy(c, p, side).start()

    def pass_on(c):
        @pl.when(jnp.logical_and(first, c + FIRST_AHEAD < chunks))
        def _():
            pass_first(c + FIRST_AHEAD)

        @pl.when(jnp.logical_and(later_even, c + EVEN_AHEAD < chunks))
        def _():
            pass_even(c + EVEN_AHEAD)

    @pl.when(first)
    def _():
        for c in range(chunks):
            load_copy(c).start()
        for c in range(FIRST_AHEAD):
            pass_first(c)

    @pl.when(later_even)
    def _():
        for c in range(EVEN_AHEAD):
            pass_even(c)

    @pl.loop(0, chunks)
    def _(c):
        if PASS_AT == 0:
            pass_on(c)

        whole = jnp.logical_or(c < DIRECT_HEAD, c >= chunks - DIRECT_TAIL)

        @pl.when(jnp.logical_or(odd, jnp.logical_and(later_even, whole)))
        def _():
            for p in range(pieces):
                down_copy(c, p).wait_recv()

        for p in range(pieces):
            for side in range(2):
                pass_copy(c, p, side).wait_recv()

        @pl.when(c == 0)
        def _():
            for j in range(blocks):
                weight_copy(j).wait()

        for side in range(3):
            for b in range(blocks):
                work[side * blocks + b] = landing[c, side, :, b * width : (b + 1) * width]

        for p in range(pieces):
            for j in range(p * per_piece, (p + 1) * per_piece):
                picked = jnp.concatenate([work[ids[j, k]] for k in range(entries)], axis=1)
                summed = jnp.dot(
                    picked, held[j].reshape(entries * width, width), preferred_element_type=jnp.float32
                )
                summed = summed + bias_ref[:, j * width : (j + 1) * width]
                result[c, :, j * width : (j + 1) * width] = jnp.maximum(summed, 0.0).astype(jnp.bfloat16)

            @pl.when(section < sections - 1)
            def _():
                down_copy(c, p).start()

            for side in range(2):
                @pl.when(sends_side(c, side))
                def _():
                    down_side_copy(c, p, side).start()

            if PASS_AT == p + 1:
                pass_on(c)

        out_copy(c).start()

    @pl.loop(0, chunks)
    def _(c):
        out_copy(c).wait()
        for p in range(pieces):
            for side in range(2):
                @pl.when(jnp.logical_or(first, jnp.logical_and(later_even, passes(c, side))))
                def _():
                    pass_copy(c, p, side).wait_send()

                @pl.when(sends_side(c, side))
                def _():
                    down_side_copy(c, p, side).wait_send()

            @pl.when(section < sections - 1)
            def _():
                down_copy(c, p).wait_send()


def per_device(sections, groups, inputs, weights, pattern, bias):
    micro, batch, columns = inputs.shape
    blocks, entries, width = weights.shape[1:4]
    rows = CHUNK
    chunks = micro * batch // rows
    out = pl.pallas_call(
        functools.partial(
            kernel, sections, groups, chunks, rows, blocks, entries, width, PIECES
        ),
        out_shape=jax.ShapeDtypeStruct((micro * batch, columns), jnp.bfloat16),
        in_specs=[
            pl.BlockSpec(memory_space=pltpu.SMEM),
            pl.BlockSpec(memory_space=pltpu.VMEM),
            pl.BlockSpec(memory_space=pl.ANY),
            pl.BlockSpec(memory_space=pl.ANY),
        ],
        out_specs=pl.BlockSpec(memory_space=pl.ANY),
        scratch_shapes=[
            pltpu.SMEM((blocks, entries), jnp.int32),
            pltpu.VMEM((chunks, 3, rows, columns), jnp.bfloat16),
            pltpu.VMEM((3 * blocks, rows, width), jnp.bfloat16),
            pltpu.VMEM((blocks, entries, width, width), jnp.bfloat16),
            pltpu.VMEM((chunks, rows, columns), jnp.bfloat16),
            pltpu.SemaphoreType.DMA((blocks,)),
            pltpu.SemaphoreType.DMA((chunks,)),
            pltpu.SemaphoreType.DMA((chunks, PIECES)),
            pltpu.SemaphoreType.DMA((chunks, PIECES, 2)),
            pltpu.SemaphoreType.DMA((chunks, PIECES, 2)),
            pltpu.SemaphoreType.DMA((chunks, PIECES, 3)),
            pltpu.SemaphoreType.DMA((chunks,)),
        ],
        compiler_params=pltpu.CompilerParams(
            collective_id=0, has_side_effects=True, vmem_limit_bytes=60 << 20
        ),
        name="sections",
    )(pattern[0], bias, inputs.reshape(micro * batch, columns), weights[0])
    return out.reshape(1, micro, batch, columns)


def solution(mesh):
    return jax.shard_map(
        functools.partial(per_device, mesh.shape["pipe"], mesh.shape["neuron"]),
        mesh=mesh,
        in_specs=(
            P(None, None, "neuron"),
            P("pipe", "neuron", None, None, None),
            P("pipe", "neuron", None),
            P("pipe", "neuron"),
        ),
        out_specs=P("pipe", None, None, "neuron"),
        check_vma=False,
    )
```

time: 454 us -> 97 us (0.21)
  waiting for transfers between devices: 375 us -> 0 us
  Pallas kernels: 0 us -> 94.5 us
  starting transfers between devices: 29.2 us -> 0 us
  other arithmetic: 23.1 us -> 0 us
  local copies, waits for them, and re-layouts: 15.1 us -> 2.3 us
  matrix products: 10.6 us -> 0 us
    ppermute x24 -> x0, waiting for transfers between devices: 375 us -> none  [the longest x8 239 us: passed_along(): return lax.ppermute(shard, axis, pairs)]
    pallas_call x0 -> x1, Pallas kernels: none -> 94.5 us  [per_device(): pl.pallas_call(functools.partial(kernel, sections, groups, chunks, rows,...]
    ppermute x24 -> x0, starting transfers between devices: 29.2 us -> none  [the longest x8 10.3 us: passed_along(): return lax.ppermute(shard, axis, pairs)]
    select_n x18 -> x0, other arithmetic: 18.2 us -> none  [the longest x8 17.3 us: store(): return jnp.where(active, result, outputs)]
    dot_general x1 -> x0, matrix products: 10.6 us -> none  [layer_apply(): jnp.einsum('rjkc,jkcd->rjd', picked, weights[0], preferred_element_type=j...]
    gather x1 -> x0, local copies, waits for them, and re-layouts: 9.73 us -> none  [layer_apply(): jnp.take(tiles, local_ids, axis=1)]
  transfers between devices with their start and end apart: 24 -> 0, of which waited for: 24 -> 0; matrix products, arithmetic and copies ran while one was open for 4% -> 0% of each run, Pallas kernels for 0% -> 0%
where the time goes in v1:
time: 97 us; the launch traced here: 96.8 us
  Pallas kernels  94.5 us (97%)
  local copies, waits for them, and re-layouts  2.3 us (2%)
    pallas_call x1, Pallas kernels, per_device(): pl.pallas_call(functools.partial(kernel, sections, groups, chunks, rows,...  94.5 us
    unnamed x1, local copies, waits for them, and re-layouts  2.3 us

profile of v1, /device:TPU:7, one launch (start us, length us, event | category | flops | bytes accessed | tf_op | source)
XLA Modules:
  0.0 96.8 jit_solution(12088727701406555929)
XLA Ops:
  0.0 94.5 %sections.1 = bf16[256,2048]{1,0:T(8,128)(2,1)} custom-call(s32[16,16]{1,0:T(8,128)} %bitcast.7, f32[1,2048]{1,0:T(1,128)} %bias_ref.1, bf16[256,2048]{1,0:T(8,128)(2,1)} %bitcast.6, bf16[16,16,128,128]{3,2,1,0:T(8,128)(2,1)} %bitcast.4), custom_call_target="tpu_custom_call" | custom-call | tf_op jit(solution)/shard_map/sections/pallas_call | solution.py:259
  94.5 2.3 %copy.6 = bf16[1,2,128,2048]{3,2,1,0:T(8,128)(2,1)} copy(bf16[1,2,128,2048]{3,2,1,0:T(8,128)(2,1)} %bitcast.5) | data formatting | bytes 2097152

commit v2 on v0

v2 whole, which is shorter than its diff:
```python
import functools

import jax
import jax.numpy as jnp
from jax import lax
from jax.experimental import pallas as pl
from jax.experimental.pallas import tpu as pltpu
from jax.sharding import PartitionSpec as P

MESH = pl.DeviceIdType.MESH
UNIT = 16
OFFLOAD = 16
DIRECT_EDGE = 0
FIRST_AHEAD = 5
EVEN_AHEAD = 4
PASS_AT = 0


def kernel(
    sections, groups, units, rows, blocks, entries, width,
    pattern_hbm, bias_hbm, x_ref, w_ref, result,
    pattern_ref, bias_ref, ids, landing, work, held,
    small_sem, w_sem, in_sem, own_sem, side_sem, pass_sem, send_sem,
):
    section = lax.axis_index("pipe")
    group = lax.axis_index("neuron")
    right = lax.rem(group + 1, groups)
    left = lax.rem(group + groups - 1, groups)
    even = lax.rem(section, 2) == 0
    first = section == 0
    last = section == sections - 1
    later_even = jnp.logical_and(even, section > 0)
    odd = jnp.logical_not(even)
    odd_sends = jnp.logical_and(odd, section < sections - 1)
    beside = (group, left, right)

    barrier = pltpu.get_barrier_semaphore()

    def signal(to_section, to_group):
        pl.semaphore_signal(
            barrier, inc=1, device_id={"pipe": to_section, "neuron": to_group}, device_id_type=MESH
        )

    @pl.when(even)
    def _():
        signal(section, left)
        signal(section, right)
        for to in beside:
            signal(section + 1, to)

    @pl.when(first)
    def _():
        signal(sections - 1, left)
        signal(sections - 1, right)

    @pl.when(last)
    def _():
        signal(0, left)
        signal(0, right)

    @pl.when(later_even)
    def _():
        for to in beside:
            signal(section - 1, to)

    @pl.when(odd)
    def _():
        for to in beside:
            signal(section - 1, to)

    @pl.when(odd_sends)
    def _():
        for to in beside:
            signal(section + 1, to)

    pattern_copy = pltpu.make_async_copy(pattern_hbm, pattern_ref, small_sem.at[0])
    bias_copy = pltpu.make_async_copy(bias_hbm, bias_ref, small_sem.at[1])
    pattern_copy.start()
    bias_copy.start()

    def unit_rows(u):
        return pl.ds(pl.multiple_of(u * rows, rows), rows)

    def load_copy(u):
        return pltpu.make_async_copy(x_ref.at[unit_rows(u)], landing.at[1, unit_rows(u)], in_sem.at[u])

    def weight_copy(j):
        return pltpu.make_async_copy(w_ref.at[j], held.at[j], w_sem.at[j])

    @pl.when(first)
    def _():
        for u in range(units):
            load_copy(u).start()

    for j in range(blocks):
        weight_copy(j).start()

    @pl.when(first)
    def _():
        pl.semaphore_wait(barrier, 7)

    @pl.when(later_even)
    def _():
        pl.semaphore_wait(barrier, 8)

    @pl.when(odd_sends)
    def _():
        pl.semaphore_wait(barrier, 6)

    @pl.when(last)
    def _():
        pl.semaphore_wait(barrier, 5)

    def remote(src, dst, send, recv, to_section, to_group):
        return pltpu.make_async_remote_copy(
            src_ref=src, dst_ref=dst, send_sem=send, recv_sem=recv,
            device_id={"pipe": to_section, "neuron": to_group}, device_id_type=MESH,
        )

    def pass_copy(u, side):
        return remote(
            landing.at[1, unit_rows(u)], landing.at[2 * side, unit_rows(u)],
            pass_sem.at[u, side], side_sem.at[u, side], section, (right, left)[side],
        )

    def input_copy(u, side):
        return remote(
            x_ref.at[unit_rows(u)], landing.at[2 * side, unit_rows(u)],
            pass_sem.at[u, side], side_sem.at[u, side], 0, (right, left)[side],
        )

    def down_copy(u):
        return remote(
            result.at[unit_rows(u)], landing.at[1, unit_rows(u)],
            send_sem.at[u, 2], own_sem.at[u], section + 1, group,
        )

    def down_side_copy(u, side):
        return remote(
            result.at[unit_rows(u)], landing.at[2 * side, unit_rows(u)],
            send_sem.at[u, side], side_sem.at[u, side], section + 1, (right, left)[side],
        )

    def direct(side):
        if not DIRECT_EDGE:
            return section < 0
        return lax.rem((group, left)[side], DIRECT_EDGE) == DIRECT_EDGE - 1

    passes = [jnp.logical_and(later_even, jnp.logical_not(direct(side))) for side in range(2)]
    sends_side = [jnp.logical_or(even, jnp.logical_and(odd_sends, direct(side))) for side in range(2)]

    def pass_first(u):
        for side in range(2):
            pass_copy(u, side).start()

    def pass_even(u):
        down_copy(u).wait_recv()
        for side in range(2):
            @pl.when(passes[side])
            def _():
                pass_copy(u, side).start()

    def pass_on(u):
        if OFFLOAD > FIRST_AHEAD:
            @pl.when(jnp.logical_and(first, u + FIRST_AHEAD < OFFLOAD))
            def _():
                pass_first(u + FIRST_AHEAD)

        @pl.when(jnp.logical_and(later_even, u + EVEN_AHEAD < units))
        def _():
            pass_even(u + EVEN_AHEAD)

    @pl.when(first)
    def _():
        for u in range(min(FIRST_AHEAD, OFFLOAD)):
            load_copy(u).wait()
            pass_first(u)
        for u in range(min(FIRST_AHEAD, OFFLOAD), units):
            load_copy(u).wait()

    @pl.when(last)
    def _():
        for u in range(OFFLOAD, units):
            for side in range(2):
                input_copy(u, side).start()

    pattern_copy.wait()
    base = (group - 1) * blocks
    total = groups * blocks

    @pl.loop(0, blocks)
    def _(j):
        for k in range(entries):
            near = lax.rem(pattern_ref[j, k] - base + total, total)
            ids[j, k] = jnp.minimum(near, 3 * blocks - 1)

    @pl.when(later_even)
    def _():
        for u in range(EVEN_AHEAD):
            pass_even(u)

    @pl.loop(0, units)
    def _(u):
        if not PASS_AT:
            pass_on(u)

        @pl.when(odd)
        def _():
            down_copy(u).wait_recv()

        for side in range(2):
            pass_copy(u, side).wait_recv()

        @pl.when(u == 0)
        def _():
            bias_copy.wait()
            for j in range(blocks):
                weight_copy(j).wait()

        for side in range(3):
            for b in range(blocks):
                work[side * blocks + b] = landing[side, unit_rows(u), b * width : (b + 1) * width]

        for j in range(blocks):
            if PASS_AT and j == PASS_AT:
                pass_on(u)
            picked = jnp.concatenate([work[ids[j, k]] for k in range(entries)], axis=1)
            summed = jnp.dot(
                picked, held[j].reshape(entries * width, width), preferred_element_type=jnp.float32
            )
            summed = summed + bias_ref[:, j * width : (j + 1) * width]
            result[unit_rows(u), j * width : (j + 1) * width] = jnp.maximum(summed, 0.0).astype(jnp.bfloat16)

        for side in range(2):
            @pl.when(sends_side[side])
            def _():
                down_side_copy(u, side).start()

        @pl.when(jnp.logical_not(last))
        def _():
            down_copy(u).start()

    def drain_side(u, side):
        @pl.when(jnp.logical_or(jnp.logical_and(first, u < OFFLOAD), passes[side]))
        def _():
            pass_copy(u, side).wait_send()

        @pl.when(sends_side[side])
        def _():
            down_side_copy(u, side).wait_send()

    @pl.when(jnp.logical_not(last))
    def _():
        @pl.loop(0, units)
        def _(u):
            drain_side(u, 0)
            drain_side(u, 1)
            down_copy(u).wait_send()

    if OFFLOAD < units:
        @pl.when(last)
        def _():
            @pl.loop(OFFLOAD, units)
            def _(u):
                input_copy(u, 0).wait_send()
                input_copy(u, 1).wait_send()


def per_device(sections, groups, inputs, weights, pattern, bias):
    micro, batch, columns = inputs.shape
    blocks, entries, width = weights.shape[1:4]
    units = micro * batch // UNIT
    dma = pltpu.SemaphoreType.DMA
    out = pl.pallas_call(
        functools.partial(
            kernel, sections, groups, units, UNIT, blocks, entries, width
        ),
        out_shape=pltpu.VMEM((micro * batch, columns), jnp.bfloat16),
        in_specs=[pl.BlockSpec(memory_space=pl.ANY)] * 4,
        out_specs=pl.BlockSpec(memory_space=pltpu.VMEM),
        scratch_shapes=[
            pltpu.SMEM((blocks, entries), jnp.int32),
            pltpu.VMEM((1, columns), jnp.float32),
            pltpu.SMEM((blocks, entries), jnp.int32),
            pltpu.VMEM((3, micro * batch, columns), jnp.bfloat16),
            pltpu.VMEM((3 * blocks, UNIT, width), jnp.bfloat16),
            pltpu.VMEM((blocks, entries, width, width), jnp.bfloat16),
            dma((2,)),
            dma((blocks,)),
            dma((units,)),
            dma((units,)),
            dma((units, 2)),
            dma((units, 2)),
            dma((units, 3)),
        ],
        compiler_params=pltpu.CompilerParams(
            collective_id=0, has_side_effects=True, vmem_limit_bytes=60 << 20
        ),
        name="sections",
    )(pattern[0], bias, inputs.reshape(micro * batch, columns), weights[0])
    return out.reshape(1, micro, batch, columns)


def solution(mesh):
    return jax.shard_map(
        functools.partial(per_device, mesh.shape["pipe"], mesh.shape["neuron"]),
        mesh=mesh,
        in_specs=(
            P(None, None, "neuron"),
            P("pipe", "neuron", None, None, None),
            P("pipe", "neuron", None),
            P("pipe", "neuron"),
        ),
        out_specs=P("pipe", None, None, "neuron"),
        check_vma=False,
    )
```

time: 454 us -> 91.6 us (0.20)
  waiting for transfers between devices: 375 us -> 0 us
  Pallas kernels: 0 us -> 90.6 us
  starting transfers between devices: 29.2 us -> 0 us
  other arithmetic: 23.1 us -> 0 us
  local copies, waits for them, and re-layouts: 15.1 us -> 0.97 us
  matrix products: 10.6 us -> 0 us
    ppermute x24 -> x0, waiting for transfers between devices: 375 us -> none  [the longest x8 239 us: passed_along(): return lax.ppermute(shard, axis, pairs)]
    pallas_call x0 -> x1, Pallas kernels: none -> 90.6 us  [per_device(): pl.pallas_call(functools.partial(kernel, sections, groups, units, UNIT, b...]
    ppermute x24 -> x0, starting transfers between devices: 29.2 us -> none  [the longest x8 10.3 us: passed_along(): return lax.ppermute(shard, axis, pairs)]
    select_n x18 -> x0, other arithmetic: 18.2 us -> none  [the longest x8 17.3 us: store(): return jnp.where(active, result, outputs)]
    dot_general x1 -> x0, matrix products: 10.6 us -> none  [layer_apply(): jnp.einsum('rjkc,jkcd->rjd', picked, weights[0], preferred_element_type=j...]
    gather x1 -> x0, local copies, waits for them, and re-layouts: 9.73 us -> none  [layer_apply(): jnp.take(tiles, local_ids, axis=1)]
  transfers between devices with their start and end apart: 24 -> 0, of which waited for: 24 -> 0; matrix products, arithmetic and copies ran while one was open for 4% -> 0% of each run, Pallas kernels for 0% -> 0%
where the time goes in v2:
time: 91.6 us
  Pallas kernels  90.6 us (99%)
  local copies, waits for them, and re-layouts  0.97 us (1%)
    pallas_call x1, Pallas kernels, per_device(): pl.pallas_call(functools.partial(kernel, sections, groups, units, UNIT, b...  90.6 us

profile of v2, /device:TPU:7, one launch (start us, length us, event | category | flops | bytes accessed | tf_op | source)
XLA Modules:
  0.0 91.6 jit_solution(16205117220308552786)
XLA Ops:
  0.0 90.6 %sections.1 = bf16[256,2048]{1,0:T(8,128)(2,1)S(1)} custom-call(s32[16,16]{1,0:T(8,128)} %bitcast.7, f32[1,2048]{1,0:T(1,128)} %bias_hbm.1, bf16[256,2048]{1,0:T(8,128)(2,1)} %bitcast.6, bf16[16,16,128,128]{3,2,1,0:T(8,128)(2,1)} %bitcast.5), custom_call_target="tpu_custom_call" | custom-call | tf_op jit(solution)/shard_map/sections/pallas_call | solution.py:274
  90.6 1.0 %copy.6 = bf16[1,2,128,2048]{3,2,1,0:T(8,128)(2,1)} copy(bf16[1,2,128,2048]{3,2,1,0:T(8,128)(2,1)S(1)} %bitcast.4) | data formatting | bytes 2097152

commit v3 on v2

--- a/solution.py
+++ b/solution.py
@@ -9,11 +9,11 @@
 
 MESH = pl.DeviceIdType.MESH
 UNIT = 16
-OFFLOAD = 16
-DIRECT_EDGE = 0
+DIRECT_EDGE = 32
+OFFLOAD = 2
 FIRST_AHEAD = 5
 EVEN_AHEAD = 4
-PASS_AT = 0
+NEAR_AHEAD = 2
 
 
 def kernel(
@@ -141,17 +141,19 @@
             send_sem.at[u, side], side_sem.at[u, side], section + 1, (right, left)[side],
         )
 
-    def direct(side):
-        if not DIRECT_EDGE:
-            return section < 0
-        return lax.rem((group, left)[side], DIRECT_EDGE) == DIRECT_EDGE - 1
-
-    passes = [jnp.logical_and(later_even, jnp.logical_not(direct(side))) for side in range(2)]
-    sends_side = [jnp.logical_or(even, jnp.logical_and(odd_sends, direct(side))) for side in range(2)]
+    direct = [lax.rem(border, DIRECT_EDGE) == DIRECT_EDGE - 1 for border in (group, left)]
+    near = jnp.logical_or(direct[0], direct[1])
+    passes = [jnp.logical_and(later_even, jnp.logical_not(direct[side])) for side in range(2)]
+    sends_side = [jnp.logical_or(even, jnp.logical_and(odd_sends, direct[side])) for side in range(2)]
+
+    def by_first(u, side):
+        return jnp.logical_or(u < OFFLOAD, jnp.logical_not(direct[side]))
 
     def pass_first(u):
         for side in range(2):
-            pass_copy(u, side).start()
+            @pl.when(by_first(u, side))
+            def _():
+                pass_copy(u, side).start()
 
     def pass_even(u):
         down_copy(u).wait_recv()
@@ -161,28 +163,30 @@
                 pass_copy(u, side).start()
 
     def pass_on(u):
-        if OFFLOAD > FIRST_AHEAD:
-            @pl.when(jnp.logical_and(first, u + FIRST_AHEAD < OFFLOAD))
-            def _():
-                pass_first(u + FIRST_AHEAD)
-
-        @pl.when(jnp.logical_and(later_even, u + EVEN_AHEAD < units))
-        def _():
-            pass_even(u + EVEN_AHEAD)
+        @pl.when(jnp.logical_and(first, u + FIRST_AHEAD < units))
+        def _():
+            pass_first(u + FIRST_AHEAD)
+
+        for some, ahead in ((near, NEAR_AHEAD), (jnp.logical_not(near), EVEN_AHEAD)):
+            @pl.when(jnp.logical_and(jnp.logical_and(later_even, some), u + ahead < units))
+            def _():
+                pass_even(u + ahead)
 
     @pl.when(first)
     def _():
-        for u in range(min(FIRST_AHEAD, OFFLOAD)):
+        for u in range(FIRST_AHEAD):
             load_copy(u).wait()
             pass_first(u)
-        for u in range(min(FIRST_AHEAD, OFFLOAD), units):
+        for u in range(FIRST_AHEAD, units):
             load_copy(u).wait()
 
     @pl.when(last)
     def _():
-        for u in range(OFFLOAD, units):
-            for side in range(2):
-                input_copy(u, side).start()
+        for side in range(2):
+            @pl.when(direct[side])
+            def _():
+                for u in range(OFFLOAD, units):
+                    input_copy(u, side).start()
 
     pattern_copy.wait()
     base = (group - 1) * blocks
@@ -196,13 +200,17 @@
 
     @pl.when(later_even)
     def _():
-        for u in range(EVEN_AHEAD):
+        for u in range(NEAR_AHEAD):
             pass_even(u)
+
+        @pl.when(jnp.logical_not(near))
+        def _():
+            for u in range(NEAR_AHEAD, EVEN_AHEAD):
+                pass_even(u)
 
     @pl.loop(0, units)
     def _(u):
-        if not PASS_AT:
-            pass_on(u)
+        pass_on(u)
 
         @pl.when(odd)
         def _():
@@ -222,8 +230,6 @@
                 work[side * blocks + b] = landing[side, unit_rows(u), b * width : (b + 1) * width]
 
         for j in range(blocks):
-            if PASS_AT and j == PASS_AT:
-                pass_on(u)
             picked = jnp.concatenate([work[ids[j, k]] for k in range(entries)], axis=1)
             summed = jnp.dot(
                 picked, held[j].reshape(entries * width, width), preferred_element_type=jnp.float32
@@ -231,17 +237,21 @@
             summed = summed + bias_ref[:, j * width : (j + 1) * width]
             result[unit_rows(u), j * width : (j + 1) * width] = jnp.maximum(summed, 0.0).astype(jnp.bfloat16)
 
+        @pl.when(odd_sends)
+        def _():
+            down_copy(u).start()
+
         for side in range(2):
             @pl.when(sends_side[side])
             def _():
                 down_side_copy(u, side).start()
 
-        @pl.when(jnp.logical_not(last))
+        @pl.when(even)
         def _():
             down_copy(u).start()
 
     def drain_side(u, side):
-        @pl.when(jnp.logical_or(jnp.logical_and(first, u < OFFLOAD), passes[side]))
+        @pl.when(jnp.logical_or(jnp.logical_and(first, by_first(u, side)), passes[side]))
         def _():
             pass_copy(u, side).wait_send()
 
@@ -257,13 +267,14 @@
             drain_side(u, 1)
             down_copy(u).wait_send()
 
-    if OFFLOAD < units:
-        @pl.when(last)
-        def _():
-            @pl.loop(OFFLOAD, units)
-            def _(u):
-                input_copy(u, 0).wait_send()
-                input_copy(u, 1).wait_send()
+    @pl.when(last)
+    def _():
+        for side in range(2):
+            @pl.when(direct[side])
+            def _():
+                @pl.loop(OFFLOAD, units)
+                def _(u):
+                    input_copy(u, side).wait_send()
 
 
 def per_device(sections, groups, inputs, weights, pattern, bias):

time: 91.6 us -> 88.4 us (0.965)
  Pallas kernels: 90.6 us -> 87.4 us
    pallas_call x1, Pallas kernels: 90.6 us -> 87.4 us  [per_device(): pl.pallas_call(functools.partial(kernel, sections, groups, units, UNIT, b...]
where the time goes in v3:
time: 88.4 us; the launch traced here: 88.3 us
  Pallas kernels  87.4 us (99%)
  local copies, waits for them, and re-layouts  0.97 us (1%)
    pallas_call x1, Pallas kernels, per_device(): pl.pallas_call(functools.partial(kernel, sections, groups, units, UNIT, b...  87.4 us

profile of v3, /device:TPU:7, one launch (start us, length us, event | category | flops | bytes accessed | tf_op | source)
XLA Modules:
  0.0 88.3 jit_solution(18144793746549352498)
XLA Ops:
  0.0 87.4 %sections.1 = bf16[256,2048]{1,0:T(8,128)(2,1)S(1)} custom-call(s32[16,16]{1,0:T(8,128)} %bitcast.7, f32[1,2048]{1,0:T(1,128)} %bias_hbm.1, bf16[256,2048]{1,0:T(8,128)(2,1)} %bitcast.6, bf16[16,16,128,128]{3,2,1,0:T(8,128)(2,1)} %bitcast.5), custom_call_target="tpu_custom_call" | custom-call | tf_op jit(solution)/shard_map/sections/pallas_call | solution.py:285
  87.4 1.0 %copy.6 = bf16[1,2,128,2048]{3,2,1,0:T(8,128)(2,1)} copy(bf16[1,2,128,2048]{3,2,1,0:T(8,128)(2,1)S(1)} %bitcast.4) | data formatting | bytes 2097152

commit v4 on v3

--- a/solution.py
+++ b/solution.py
@@ -34,6 +34,9 @@
     odd_sends = jnp.logical_and(odd, section < sections - 1)
     beside = (group, left, right)
 
+    direct = [lax.rem(border, DIRECT_EDGE) == DIRECT_EDGE - 1 for border in (group, left)]
+    near = jnp.logical_or(direct[0], direct[1])
+
     barrier = pltpu.get_barrier_semaphore()
 
     def signal(to_section, to_group):
@@ -48,30 +51,27 @@
         for to in beside:
             signal(section + 1, to)
 
-    @pl.when(first)
-    def _():
-        signal(sections - 1, left)
-        signal(sections - 1, right)
-
-    @pl.when(last)
-    def _():
-        signal(0, left)
-        signal(0, right)
-
     @pl.when(later_even)
+    def _():
+        signal(section - 1, group)
+
+    @pl.when(odd)
     def _():
         for to in beside:
             signal(section - 1, to)
 
-    @pl.when(odd)
-    def _():
-        for to in beside:
-            signal(section - 1, to)
-
     @pl.when(odd_sends)
     def _():
-        for to in beside:
-            signal(section + 1, to)
+        signal(section + 1, group)
+
+    for side in range(2):
+        to = (right, left)[side]
+        for some, to_section in (
+            (first, sections - 1), (last, 0), (later_even, section - 1), (odd_sends, section + 1)
+        ):
+            @pl.when(jnp.logical_and(some, direct[side]))
+            def _():
+                signal(to_section, to)
 
     pattern_copy = pltpu.make_async_copy(pattern_hbm, pattern_ref, small_sem.at[0])
     bias_copy = pltpu.make_async_copy(bias_hbm, bias_ref, small_sem.at[1])
@@ -95,21 +95,14 @@
     for j in range(blocks):
         weight_copy(j).start()
 
-    @pl.when(first)
-    def _():
-        pl.semaphore_wait(barrier, 7)
-
-    @pl.when(later_even)
-    def _():
-        pl.semaphore_wait(barrier, 8)
-
-    @pl.when(odd_sends)
-    def _():
-        pl.semaphore_wait(barrier, 6)
-
-    @pl.when(last)
-    def _():
-        pl.semaphore_wait(barrier, 5)
+    for some, count in ((first, 5), (later_even, 6), (odd_sends, 4), (last, 3)):
+        @pl.when(jnp.logical_and(some, near))
+        def _():
+            pl.semaphore_wait(barrier, count + 1)
+
+        @pl.when(jnp.logical_and(some, jnp.logical_not(near)))
+        def _():
+            pl.semaphore_wait(barrier, count)
 
     def remote(src, dst, send, recv, to_section, to_group):
         return pltpu.make_async_remote_copy(
@@ -141,8 +134,6 @@
             send_sem.at[u, side], side_sem.at[u, side], section + 1, (right, left)[side],
         )
 
-    direct = [lax.rem(border, DIRECT_EDGE) == DIRECT_EDGE - 1 for border in (group, left)]
-    near = jnp.logical_or(direct[0], direct[1])
     passes = [jnp.logical_and(later_even, jnp.logical_not(direct[side])) for side in range(2)]
     sends_side = [jnp.logical_or(even, jnp.logical_and(odd_sends, direct[side])) for side in range(2)]
 

time: 88.4 us -> 88.1 us (level)
  no operation moved by 1% of the time
where the time goes in v4:
time: 88.1 us
  Pallas kernels  87.1 us (99%)
  local copies, waits for them, and re-layouts  0.97 us (1%)
    pallas_call x1, Pallas kernels, per_device(): pl.pallas_call(functools.partial(kernel, sections, groups, units, UNIT, b...  87.1 us

profile of v4, /device:TPU:7, one launch (start us, length us, event | category | flops | bytes accessed | tf_op | source)
XLA Modules:
  0.0 88.1 jit_solution(11247766436655586194)
XLA Ops:
  0.0 87.1 %sections.1 = bf16[256,2048]{1,0:T(8,128)(2,1)S(1)} custom-call(s32[16,16]{1,0:T(8,128)} %bitcast.7, f32[1,2048]{1,0:T(1,128)} %bias_hbm.1, bf16[256,2048]{1,0:T(8,128)(2,1)} %bitcast.6, bf16[16,16,128,128]{3,2,1,0:T(8,128)(2,1)} %bitcast.5), custom_call_target="tpu_custom_call" | custom-call | tf_op jit(solution)/shard_map/sections/pallas_call | solution.py:276
  87.1 1.0 %copy.6 = bf16[1,2,128,2048]{3,2,1,0:T(8,128)(2,1)} copy(bf16[1,2,128,2048]{3,2,1,0:T(8,128)(2,1)S(1)} %bitcast.4) | data formatting | bytes 2097152

commit v5 on v4

--- a/solution.py
+++ b/solution.py
@@ -11,7 +11,7 @@
 UNIT = 16
 DIRECT_EDGE = 32
 OFFLOAD = 2
-FIRST_AHEAD = 5
+FIRST_AHEAD = 4
 EVEN_AHEAD = 4
 NEAR_AHEAD = 2
 
@@ -179,6 +179,10 @@
                 for u in range(OFFLOAD, units):
                     input_copy(u, side).start()
 
+                @pl.loop(OFFLOAD, units)
+                def _(u):
+                    input_copy(u, side).wait_send()
+
     pattern_copy.wait()
     base = (group - 1) * blocks
     total = groups * blocks
@@ -257,15 +261,6 @@
             drain_side(u, 0)
             drain_side(u, 1)
             down_copy(u).wait_send()
-
-    @pl.when(last)
-    def _():
-        for side in range(2):
-            @pl.when(direct[side])
-            def _():
-                @pl.loop(OFFLOAD, units)
-                def _(u):
-                    input_copy(u, side).wait_send()
 
 
 def per_device(sections, groups, inputs, weights, pattern, bias):

time: 88.1 us -> 88.2 us (level)
  no operation moved by 1% of the time
where the time goes in v5:
time: 88.2 us; the launch traced here: 88.1 us
  Pallas kernels  87.1 us (99%)
  local copies, waits for them, and re-layouts  0.97 us (1%)
    pallas_call x1, Pallas kernels, per_device(): pl.pallas_call(functools.partial(kernel, sections, groups, units, UNIT, b...  87.1 us

profile of v5, /device:TPU:7, one launch (start us, length us, event | category | flops | bytes accessed | tf_op | source)
XLA Modules:
  0.0 88.1 jit_solution(336839433719253975)
XLA Ops:
  0.0 87.1 %sections.1 = bf16[256,2048]{1,0:T(8,128)(2,1)S(1)} custom-call(s32[16,16]{1,0:T(8,128)} %bitcast.7, f32[1,2048]{1,0:T(1,128)} %bias_hbm.1, bf16[256,2048]{1,0:T(8,128)(2,1)} %bitcast.6, bf16[16,16,128,128]{3,2,1,0:T(8,128)(2,1)} %bitcast.5), custom_call_target="tpu_custom_call" | custom-call | tf_op jit(solution)/shard_map/sections/pallas_call | solution.py:271
  87.1 1.0 %copy.6 = bf16[1,2,128,2048]{3,2,1,0:T(8,128)(2,1)} copy(bf16[1,2,128,2048]{3,2,1,0:T(8,128)(2,1)S(1)} %bitcast.4) | data formatting | bytes 2097152
